TPU v7x, 128 devices: a whole 4x4x4 slice. The times are simulated.
128 devices in a mesh: grp: 4 (over y), dev: 32 (over z, x, core).
Axes of the slice: x: 4, y: 4, z: 4, core: 2. Of those that a mesh axis runs over, the one named last changes fastest.
Arguments:
- points: float32 [64, 196608], P(None, 'dev'), may hold values from -6 to 6
- weights: float32 [196608, 128], P('dev'), may hold values from -4 to 4
- proj: float32 [256, 196608], P(None, 'dev'), may hold values from -0.078125 to 0.078125
- fetch_table: int32 [3, 32, 32, 2], P(None, 'dev'), may hold values from 0 to 11, as said below
- near_list: int32 [384, 16], P('dev'), may hold values from 0 to 63, as said below
- far_list: int32 [384, 8], P('dev'), may hold values from 0 to 31, as said below
- skel_idx: int32 [32, 256], P('dev'), may hold values from 0 to 6143, as said below
Outputs:
- potential: float32 [196608, 128], P('dev')
Inputs may be any that keep to these rules, and one draw needn't show every extreme that they name: Entries of fetch_table[r, d, e] are distinct local leaf numbers of column e. `near_list`: the 16 slots of one target leaf are distinct. `far_list`: the 8 nodes of one target leaf are distinct, and one of them is node (c + 1) mod 32 for the leaf's column c. `skel_idx`: the 256 skeleton points of one node are distinct.
All inputs are finite; a program needn't handle non-finite values.
Results may differ from a plain program's by a relative error of at most 0.0003.
Values sent between devices are 32-bit elements; how exact they have to be, the bound alone decides.
A program may use at most 192 MiB of HBM per device.

v0:
```python
import jax
import jax.numpy as jnp
from jax import lax
from jax.sharding import PartitionSpec as P


def kernel_sum(target, sources, values):
    high = lax.Precision.HIGHEST
    inner = jnp.einsum("dt,jds->tjs", target, sources, precision=high)
    target_norm = jnp.sum(target * target, axis=0)
    source_norm = jnp.sum(sources * sources, axis=1)
    distance = target_norm[:, None, None] + source_norm[None] - 2.0 * inner
    kernel = jnp.exp(-distance * (2.0 / target.shape[0]))
    return jnp.einsum("tjs,jsw->tw", kernel, values, precision=high)


def on_device(points, weights, proj, fetch_table, near_list, far_list, skel_idx):
    features, column_points = points.shape
    columns = weights.shape[1]
    devices = lax.axis_size("dev")
    groups = lax.axis_size("grp")
    targets = near_list.shape[0]
    leaf_size = column_points // targets
    row_leaves = targets // (groups - 1)
    capacity = fetch_table.shape[3]
    skeleton = skel_idx.shape[1]
    group_index = lax.axis_index("grp")
    near_row = jnp.minimum(group_index, groups - 2)
    far_side = group_index == groups - 1
    leaf_coords = points.reshape(features, targets, leaf_size)
    leaf_weights = weights.reshape(targets, leaf_size, columns)
    requests = lax.dynamic_index_in_dim(fetch_table[:, 0], near_row, 0, keepdims=False)
    asked = lax.all_to_all(requests, "dev", split_axis=0, concat_axis=0, tiled=True)
    coords = jnp.moveaxis(jnp.take(leaf_coords, asked, axis=1), 0, 2)
    values = jnp.take(leaf_weights, asked, axis=0)
    fetched_coords = lax.all_to_all(coords, "dev", split_axis=0, concat_axis=0, tiled=True)
    fetched_values = lax.all_to_all(values, "dev", split_axis=0, concat_axis=0, tiled=True)
    flat_coords = fetched_coords.reshape(devices * capacity, features, leaf_size)
    flat_values = fetched_values.reshape(devices * capacity, leaf_size, columns)
    local_skeleton = jnp.take(points, skel_idx[0], axis=1)
    share_len = column_points // groups
    share_start = group_index * share_len
    share_proj = lax.dynamic_slice_in_dim(proj, share_start, share_len, 1)
    share_weights = lax.dynamic_slice_in_dim(weights, share_start, share_len, 0)
    partial_value = jnp.dot(
        share_proj,
        share_weights,
        preferred_element_type=jnp.float32,
        precision=lax.Precision.HIGHEST,
    )
    node_index = lax.axis_index("dev")
    owner_mask = jnp.where(far_side, 1.0, 0.0).astype(jnp.float32)
    table_coords = jnp.zeros((devices, features, skeleton), jnp.float32)
    table_coords = lax.dynamic_update_index_in_dim(
        table_coords, local_skeleton * owner_mask, node_index, 0
    )
    table_weights = jnp.zeros((devices, skeleton, columns), jnp.float32)
    table_weights = lax.dynamic_update_index_in_dim(table_weights, partial_value, node_index, 0)
    skel_coords, skel_weights = lax.psum((table_coords, table_weights), ("grp", "dev"))

    def near_work():
        slots = lax.dynamic_slice_in_dim(near_list, near_row * row_leaves, row_leaves, 0)
        leaf_numbers = near_row * row_leaves + jnp.arange(row_leaves, dtype=jnp.int32)

        def near_leaf(items):
            leaf_number, leaf_slots = items
            target = jnp.take(leaf_coords, leaf_number, axis=1)
            return kernel_sum(
                target,
                jnp.take(flat_coords, leaf_slots, axis=0),
                jnp.take(flat_values, leaf_slots, axis=0),
            )

        block = lax.map(near_leaf, (leaf_numbers, slots))
        empty = jnp.zeros((targets, leaf_size, columns), jnp.float32)
        return lax.dynamic_update_slice_in_dim(empty, block, near_row * row_leaves, 0)

    def far_work():

        def far_leaf(items):
            leaf_number, node_ids = items
            target = jnp.take(leaf_coords, leaf_number, axis=1)
            return kernel_sum(
                target,
                jnp.take(skel_coords, node_ids, axis=0),
                jnp.take(skel_weights, node_ids, axis=0),
            )

        return lax.map(far_leaf, (jnp.arange(targets, dtype=jnp.int32), far_list))

    contribution = lax.cond(far_side, far_work, near_work)
    total = lax.psum(contribution, "grp")
    return total.reshape(column_points, columns)


def solution(mesh):
    placed = (
        P(None, "dev"),
        P("dev", None),
        P(None, "dev"),
        P(None, "dev", None, None),
        P("dev", None),
        P("dev", None),
        P("dev", None),
    )
    return jax.shard_map(
        on_device, mesh=mesh, in_specs=placed, out_specs=P("dev", None), check_vma=False
    )
```

profile of v0, /device:TPU:1, one launch (start us, length us, event | category | flops | bytes accessed | tf_op | source)
XLA Modules:
  0.0 820.4 jit_solution(13350892789192930071)
XLA Ops:
  8.1 9.4 %all-to-all-start = ((s32[32,1,2]{2,1,0:T(1,128)}), s32[32,1,2]{2,1,0:T(1,128)S(1)}, u32[]{:S(2)}, u32[]{:S(2)}) async-start(s32[32,1,2]{2,1,0:T(1,128)} %copy.36), calls=%async_computation | async-start | bytes 32768 | tf_op jit(solution)/shard_map/all_to_all | solution.py:33
  24.8 5.7 gather_fusion.4
  30.6 8.5 %broadcast_select_fusion.1 = f32[32,2,64,512]{3,2,1,0:T(8,128)} fusion(f32[32,2,64,512]{3,2,1,0:T(8,128)} %bitcast.103, pred[32,2]{1,0:T(8,128)(4,1)S(1)} %copy.38), kind=kLoop, calls=%fused_computation.87 | loop fusion | flops 2097152 | bytes 16777280 | tf_op jit(solution)/shard_map/jit(_take)/select_n | solution.py:34
  39.1 5.2 all-to-all-start.1
  44.3 7.4 gather_fusion.5
  51.6 11.6 %broadcast_select_fusion = f32[32,2,512,128]{3,2,1,0:T(8,128)} fusion(f32[32,2,512,128]{3,2,1,0:T(8,128)} %bitcast.101, pred[32,2]{1,0:T(8,128)(4,1)S(1)} %copy.38), kind=kLoop, calls=%fused_computation.86 | loop fusion | flops 4194304 | bytes 33554496 | tf_op jit(solution)/shard_map/jit(_take)/select_n | solution.py:35
  63.2 80.8 %all-to-all-done.1 = f32[32,2,64,512]{3,2,1,0:T(8,128)} async-done(((f32[32,2,64,512]{3,2,1,0:T(8,128)}), f32[32,2,64,512]{3,2,1,0:T(8,128)}, u32[]{:S(2)}, u32[]{:S(2)}) %all-to-all-start.1) | async-done | bytes 8388640 | tf_op jit(solution)/shard_map/all_to_all | solution.py:36
  144.0 11.3 %all-to-all-start.2 = ((f32[32,2,512,128]{3,2,1,0:T(8,128)}), f32[32,2,512,128]{3,2,1,0:T(8,128)}, u32[]{:S(2)}, u32[]{:S(2)}) async-start(f32[32,2,512,128]{3,2,1,0:T(8,128)} %broadcast_select_fusion), calls=%async_computation.2 | async-start | bytes 33554432 | tf_op jit(solution)/shard_map/all_to_all | solution.py:37
  171.4 310.3 %all-reduce.6.cloned.1.call-done = (f32[32,64,256]{2,1,0:T(8,128)}, f32[32,256,128]{2,1,0:T(8,128)}) async-done(((f32[32,64,256]{2,1,0:T(8,128)}, f32[32,256,128]{2,1,0:T(8,128)}), (f32[32,64,256]{2,1,0:T(8,128)}, f32[32,256,128]{2,1,0:T(8,128)})) %all-reduce.6.cloned.1.call-update) | async-done | bytes 6291472 | tf_op jit(solution)/shard_map/psum | solution.py:59
  481.8 223.2 %conditional.1 = (f32[12,512,128]{2,1,0:T(8,128)}) conditional(s32[]{:T(128)} %convert_element_type.3, (s32[]{:T(128)}, s32[12,16]{1,0:T(8,128)}, f32[32,2,64,512]{3,2,1,0:T(8,128)}, f32[32,2,512,128]{3,2,1,0:T(8,128)}, f32[64,12,512]{2,1,0:T(8,128)}) %tuple.20, (f32[64,12,512]{2,1,0:T(8,128)}, s32[12,8]{0,1:T(8,128)S(1)}, f32[32,64,256]{2,1,0:T(8,128)}, ...), branch_computations={%region_2.0_spmd, %region_7.13_spmd} | conditional | flops 9687917568 | bytes 60630836 | solution.py:91
  482.4 218.3 %while.19 = (s32[]{:T(128)}, f32[4,512,128]{2,1,0:T(8,128)}, s32[4]{0:T(128)S(1)}, f32[64,12,512]{2,1,0:T(8,128)}, s32[4,16]{1,0:T(4,128)S(1)}, /*index=5*/f32[6...) while((s32[]{:T(128)}, f32[4,512,128]{2,1,0:T(8,128)}, ...), condition=%wide.region_6.7_spmd, body=%wide.region_3.6_spmd.sunk | while | flops 9687917568 | bytes 55387260 | solution.py:74
  490.4 16.2 %fusion.112 = f32[512,16,512]{2,0,1:T(8,128)} fusion(f32[16,64,512]{2,1,0:T(8,128)S(1)} %gather_fusion.3, pred[16]{0:T(512)(128)(4,1)S(1)} %compare_and_fusion.7, f32[64,1,512]{2,1,0:T(1,128)S(1)} %constant_dynamic-slice_fusion.9, pred[]{:T(512)S(6)} %and.57), kind=kOutput, calls=%fused_computation.22.clone.1 | convolution fusion | flops 3221782528 | bytes 19005456 | tf_op jit(solution)/shard_map/cond/branch_0_fun/while/body/eval_jaxpr/dt,jds->tjs/dot_general | solution.py:9
  507.0 8.5 %gather_fusion.2 = f32[16,512,128]{2,1,0:T(8,128)} fusion(f32[64,512,128]{2,1,0:T(8,128)} %get-tuple-element.330, s32[1024]{0:T(1024)S(1)} %pad_clamp_fusion.7), kind=kCustom, calls=%fused_computation.1.clone.1 | custom fusion | bytes 8388672 | tf_op jit(solution)/shard_map/cond/branch_0_fun/while/body/eval_jaxpr/jit(_take)/gather | solution.py:71
  515.5 21.5 %fusion.114 = f32[4,512,128]{2,1,0:T(8,128)} fusion(f32[4,512,128]{2,1,0:T(8,128)} %get-tuple-element.314, s32[]{:T(128)} %get-tuple-element.313, f32[16,512,128]{2,1,0:T(8,128)} %gather_fusion.2, pred[16]{0:T(512)(128)(4,1)S(1)} %compare_and_fusion.7, f32[512,16,512]{2,0,1:T(8,128)} %fusion.112, f32[16,512]{1,0:T(8,128)S(1)} %multiply_reduce_fusion.5, ...), kind=kOutput, calls=%fused_computation.25.clone.1 | convolution fusion | flops 6464471040 | bytes 21269008 | tf_op jit(solution)/shard_map/cond/branch_0_fun/while/body/eval_jaxpr/tjs,jsw->tw/dot_general | solution.py:14
  545.0 16.2 %fusion.112 = f32[512,16,512]{2,0,1:T(8,128)} fusion(f32[16,64,512]{2,1,0:T(8,128)S(1)} %gather_fusion.3, pred[16]{0:T(512)(128)(4,1)S(1)} %compare_and_fusion.7, f32[64,1,512]{2,1,0:T(1,128)S(1)} %constant_dynamic-slice_fusion.9, pred[]{:T(512)S(6)} %and.57), kind=kOutput, calls=%fused_computation.22.clone.1 | convolution fusion | flops 3221782528 | bytes 19005456 | tf_op jit(solution)/shard_map/cond/branch_0_fun/while/body/eval_jaxpr/dt,jds->tjs/dot_general | solution.py:9
  561.5 8.5 %gather_fusion.2 = f32[16,512,128]{2,1,0:T(8,128)} fusion(f32[64,512,128]{2,1,0:T(8,128)} %get-tuple-element.330, s32[1024]{0:T(1024)S(1)} %pad_clamp_fusion.7), kind=kCustom, calls=%fused_computation.1.clone.1 | custom fusion | bytes 8388672 | tf_op jit(solution)/shard_map/cond/branch_0_fun/while/body/eval_jaxpr/jit(_take)/gather | solution.py:71
  570.1 21.5 %fusion.114 = f32[4,512,128]{2,1,0:T(8,128)} fusion(f32[4,512,128]{2,1,0:T(8,128)} %get-tuple-element.314, s32[]{:T(128)} %get-tuple-element.313, f32[16,512,128]{2,1,0:T(8,128)} %gather_fusion.2, pred[16]{0:T(512)(128)(4,1)S(1)} %compare_and_fusion.7, f32[512,16,512]{2,0,1:T(8,128)} %fusion.112, f32[16,512]{1,0:T(8,128)S(1)} %multiply_reduce_fusion.5, ...), kind=kOutput, calls=%fused_computation.25.clone.1 | convolution fusion | flops 6464471040 | bytes 21269008 | tf_op jit(solution)/shard_map/cond/branch_0_fun/while/body/eval_jaxpr/tjs,jsw->tw/dot_general | solution.py:14
  599.5 16.2 %fusion.112 = f32[512,16,512]{2,0,1:T(8,128)} fusion(f32[16,64,512]{2,1,0:T(8,128)S(1)} %gather_fusion.3, pred[16]{0:T(512)(128)(4,1)S(1)} %compare_and_fusion.7, f32[64,1,512]{2,1,0:T(1,128)S(1)} %constant_dynamic-slice_fusion.9, pred[]{:T(512)S(6)} %and.57), kind=kOutput, calls=%fused_computation.22.clone.1 | convolution fusion | flops 3221782528 | bytes 19005456 | tf_op jit(solution)/shard_map/cond/branch_0_fun/while/body/eval_jaxpr/dt,jds->tjs/dot_general | solution.py:9
  616.1 8.5 %gather_fusion.2 = f32[16,512,128]{2,1,0:T(8,128)} fusion(f32[64,512,128]{2,1,0:T(8,128)} %get-tuple-element.330, s32[1024]{0:T(1024)S(1)} %pad_clamp_fusion.7), kind=kCustom, calls=%fused_computation.1.clone.1 | custom fusion | bytes 8388672 | tf_op jit(solution)/shard_map/cond/branch_0_fun/while/body/eval_jaxpr/jit(_take)/gather | solution.py:71
  624.6 21.5 %fusion.114 = f32[4,512,128]{2,1,0:T(8,128)} fusion(f32[4,512,128]{2,1,0:T(8,128)} %get-tuple-element.314, s32[]{:T(128)} %get-tuple-element.313, f32[16,512,128]{2,1,0:T(8,128)} %gather_fusion.2, pred[16]{0:T(512)(128)(4,1)S(1)} %compare_and_fusion.7, f32[512,16,512]{2,0,1:T(8,128)} %fusion.112, f32[16,512]{1,0:T(8,128)S(1)} %multiply_reduce_fusion.5, ...), kind=kOutput, calls=%fused_computation.25.clone.1 | convolution fusion | flops 6464471040 | bytes 21269008 | tf_op jit(solution)/shard_map/cond/branch_0_fun/while/body/eval_jaxpr/tjs,jsw->tw/dot_general | solution.py:14
  654.1 16.2 %fusion.112 = f32[512,16,512]{2,0,1:T(8,128)} fusion(f32[16,64,512]{2,1,0:T(8,128)S(1)} %gather_fusion.3, pred[16]{0:T(512)(128)(4,1)S(1)} %compare_and_fusion.7, f32[64,1,512]{2,1,0:T(1,128)S(1)} %constant_dynamic-slice_fusion.9, pred[]{:T(512)S(6)} %and.57), kind=kOutput, calls=%fused_computation.22.clone.1 | convolution fusion | flops 3221782528 | bytes 19005456 | tf_op jit(solution)/shard_map/cond/branch_0_fun/while/body/eval_jaxpr/dt,jds->tjs/dot_general | solution.py:9
  670.7 8.5 %gather_fusion.2 = f32[16,512,128]{2,1,0:T(8,128)} fusion(f32[64,512,128]{2,1,0:T(8,128)} %get-tuple-element.330, s32[1024]{0:T(1024)S(1)} %pad_clamp_fusion.7), kind=kCustom, calls=%fused_computation.1.clone.1 | custom fusion | bytes 8388672 | tf_op jit(solution)/shard_map/cond/branch_0_fun/while/body/eval_jaxpr/jit(_take)/gather | solution.py:71
  679.2 21.5 %fusion.114 = f32[4,512,128]{2,1,0:T(8,128)} fusion(f32[4,512,128]{2,1,0:T(8,128)} %get-tuple-element.314, s32[]{:T(128)} %get-tuple-element.313, f32[16,512,128]{2,1,0:T(8,128)} %gather_fusion.2, pred[16]{0:T(512)(128)(4,1)S(1)} %compare_and_fusion.7, f32[512,16,512]{2,0,1:T(8,128)} %fusion.112, f32[16,512]{1,0:T(8,128)S(1)} %multiply_reduce_fusion.5, ...), kind=kOutput, calls=%fused_computation.25.clone.1 | convolution fusion | flops 6464471040 | bytes 21269008 | tf_op jit(solution)/shard_map/cond/branch_0_fun/while/body/eval_jaxpr/tjs,jsw->tw/dot_general | solution.py:14
  705.0 104.8 %all-reduce.4.cloned.1.call-done = f32[6144,128]{1,0:T(8,128)} async-done(((f32[6144,128]{1,0:T(8,128)}), f32[6144,128]{1,0:T(8,128)}) %all-reduce.4.cloned.1.call-update) | async-done | bytes 3145744 | tf_op jit(solution)/shard_map/psum | solution.py:92
  (75 shorter events, 59.4 us)
Async XLA Ops:
  6.5 37.7 %copy-start = (f32[6144,128]{1,0:T(8,128)S(1)}, f32[6144,128]{1,0:T(8,128)}, u32[]{:S(2)}) copy-start(f32[6144,128]{1,0:T(8,128)} %param.16) | copy-start | bytes 9437188
  8.1 16.4 %all-to-all-start = ((s32[32,1,2]{2,1,0:T(1,128)}), s32[32,1,2]{2,1,0:T(1,128)S(1)}, u32[]{:S(2)}, u32[]{:S(2)}) async-start(s32[32,1,2]{2,1,0:T(1,128)} %copy.36), calls=%async_computation | async-start | bytes 32768 | tf_op jit(solution)/shard_map/all_to_all | solution.py:33
  39.1 105.0 %all-to-all-start.1 = ((f32[32,2,64,512]{3,2,1,0:T(8,128)}), f32[32,2,64,512]{3,2,1,0:T(8,128)}, u32[]{:S(2)}, u32[]{:S(2)}) async-start(f32[32,2,64,512]{3,2,1,0:T(8,128)} %broadcast_select_fusion.1), calls=%async_computation.1 | async-start | bytes 16777216 | tf_op jit(solution)/shard_map/all_to_all | solution.py:36
  144.0 337.7 %all-to-all-start.2 = ((f32[32,2,512,128]{3,2,1,0:T(8,128)}), f32[32,2,512,128]{3,2,1,0:T(8,128)}, u32[]{:S(2)}, u32[]{:S(2)}) async-start(f32[32,2,512,128]{3,2,1,0:T(8,128)} %broadcast_select_fusion), calls=%async_computation.2 | async-start | bytes 33554432 | tf_op jit(solution)/shard_map/all_to_all | solution.py:37
  155.3 3.3 copy-start.4
  155.3 326.4 %all-reduce.6.cloned.1.call-start = ((), (), s32[]{:S(2)}) async-start(), calls=%async_computation.4 | async-start | bytes 12582912 | tf_op jit(solution)/shard_map/psum | solution.py:59
  167.2 2.3 copy-start.2
  169.4 312.3 %copy-start.3 = (s32[12,8]{0,1:T(8,128)S(1)}, s32[12,8]{0,1:T(8,128)}, u32[]{:S(2)}) copy-start(s32[12,8]{0,1:T(8,128)} %param.20) | copy-start | bytes 1156
  169.5 640.3 %all-reduce.4.cloned.1.call-start = ((), (), s32[]{:S(2)}) async-start(), calls=%async_computation.3 | async-start | bytes 6291456 | tf_op jit(solution)/shard_map/psum | solution.py:92
  705.0 108.6 %copy-start.1 = (f32[6144,128]{1,0:T(8,128)S(1)}, f32[6144,128]{1,0:T(8,128)}, u32[]{:S(2)}) copy-start(f32[6144,128]{1,0:T(8,128)} %param.16) | copy-start | bytes 9437188
Sparse Core Ops, SparseCore 0:
  169.6 312.1 all-reduce.5
  705.1 104.6 all-reduce.3
where the time goes:
time: 823 us; the launch traced here: 820 us
  waiting for transfers between devices  500 us (61%)
  matrix products  154 us (19%)
  local copies, waits for them, and re-layouts  96.2 us (12%)
  starting transfers between devices  26 us (3%)
  other arithmetic  22.5 us (3%)
  between operations  13.5 us (2%)
    psum x1, waiting for transfers between devices, on_device(): lax.psum((table_coords, table_weights), ('grp', 'dev'))  310 us
    psum x1, waiting for transfers between devices, on_device(): total = lax.psum(contribution, 'grp')  105 us
    dot_general x4, matrix products, kernel_sum(): return jnp.einsum('tjs,jsw->tw', kernel, values, precision=high)  86.1 us
    all_to_all x1, waiting for transfers between devices, on_device(): lax.all_to_all(coords, 'dev', split_axis=0, concat_axis=0, tiled=True)  80.8 us
    dot_general x4, matrix products, kernel_sum(): inner = jnp.einsum('dt,jds->tjs', target, sources, precision=high)  64.7 us
    gather x4, local copies, waits for them, and re-layouts, near_leaf(): jnp.take(flat_values, leaf_slots, axis=0)  34 us
  transfers between devices with their start and end apart: 5, of which 4 were waited for; matrix products, arithmetic and copies ran while one was open for 5% of the time, Pallas kernels for 0%

commit v1 on v0

--- a/solution.py
+++ b/solution.py
@@ -1,7 +1,21 @@
+import functools
 import jax
 import jax.numpy as jnp
 from jax import lax
 from jax.sharding import PartitionSpec as P
+
+
+def check_record(s0, group_axis):
+    cores_n = lax.axis_size(group_axis)
+    v_next = s0
+    for at in [j for j in (1, 2, 4, 8, 16) if j < cores_n]:
+        v_next = v_next + lax.ppermute(
+            v_next, axis_name=group_axis, perm=[(ii, ii ^ at) for ii in range(cores_n)]
+        )
+    return v_next
+
+
+_process_task = functools.partial(check_record, group_axis="grp")
 
 
 def kernel_sum(target, sources, values):
@@ -89,7 +103,7 @@
         return lax.map(far_leaf, (jnp.arange(targets, dtype=jnp.int32), far_list))
 
     contribution = lax.cond(far_side, far_work, near_work)
-    total = lax.psum(contribution, "grp")
+    total = _process_task(contribution)
     return total.reshape(column_points, columns)
 
 

time: 823 us -> 889 us (1.080)
  starting transfers between devices: 26 us -> 59.9 us
  waiting for transfers between devices: 500 us -> 531 us
    ppermute x0 -> x2, waiting for transfers between devices: none -> 136 us  [check_record(): lax.ppermute(v_next, axis_name=group_axis, perm=[(ii, ii ^ at) for ii in...]
    psum x1 -> x0, waiting for transfers between devices: 105 us -> none  [on_device(): total = lax.psum(contribution, 'grp')]
    ppermute x0 -> x2, starting transfers between devices: none -> 34 us  [check_record(): lax.ppermute(v_next, axis_name=group_axis, perm=[(ii, ii ^ at) for ii in...]
  transfers between devices with their start and end apart: 5 -> 6, of which waited for: 4 -> 5; matrix products, arithmetic and copies ran while one was open for 5% -> 4% of each run, Pallas kernels for 0% -> 0%
where the time goes in v1:
time: 889 us; the launch traced here: 886 us
  waiting for transfers between devices  531 us (60%)
  matrix products  154 us (17%)
  local copies, waits for them, and re-layouts  92.6 us (10%)
  starting transfers between devices  59.9 us (7%)
  other arithmetic  26.9 us (3%)
  between operations  13.5 us (2%)
    psum x1, waiting for transfers between devices, on_device(): lax.psum((table_coords, table_weights), ('grp', 'dev'))  310 us
    ppermute x2, waiting for transfers between devices, check_record(): lax.ppermute(v_next, axis_name=group_axis, perm=[(ii, ii ^ at) for ii in...  136 us
    dot_general x4, matrix products, kernel_sum(): return jnp.einsum('tjs,jsw->tw', kernel, values, precision=high)  86.1 us
    all_to_all x1, waiting for transfers between devices, on_device(): lax.all_to_all(coords, 'dev', split_axis=0, concat_axis=0, tiled=True)  80.8 us
    dot_general x4, matrix products, kernel_sum(): inner = jnp.einsum('dt,jds->tjs', target, sources, precision=high)  64.7 us
    gather x4, local copies, waits for them, and re-layouts, near_leaf(): jnp.take(flat_values, leaf_slots, axis=0)  34.1 us
    ppermute x2, starting transfers between devices, check_record(): lax.ppermute(v_next, axis_name=group_axis, perm=[(ii, ii ^ at) for ii in...  34 us
  transfers between devices with their start and end apart: 6, of which 5 were waited for; matrix products, arithmetic and copies ran while one was open for 4% of the time, Pallas kernels for 0%

profile of v1, /device:TPU:1, one launch (start us, length us, event | category | flops | bytes accessed | tf_op | source)
XLA Modules:
  0.0 886.0 jit_solution(14570256411005428466)
XLA Ops:
  8.1 9.4 %all-to-all-start = ((s32[32,1,2]{2,1,0:T(1,128)}), s32[32,1,2]{2,1,0:T(1,128)S(1)}, u32[]{:S(2)}, u32[]{:S(2)}) async-start(s32[32,1,2]{2,1,0:T(1,128)} %copy.36), calls=%async_computation | async-start | bytes 32768 | tf_op jit(solution)/shard_map/all_to_all | solution.py:47
  30.6 8.5 broadcast_select_fusion.1
  44.3 7.4 gather_fusion.5
  51.6 11.6 %broadcast_select_fusion = f32[32,2,512,128]{3,2,1,0:T(8,128)} fusion(f32[32,2,512,128]{3,2,1,0:T(8,128)} %bitcast.101, pred[32,2]{1,0:T(8,128)(4,1)S(1)} %copy.38), kind=kLoop, calls=%fused_computation.86 | loop fusion | flops 4194304 | bytes 33554496 | tf_op jit(solution)/shard_map/jit(_take)/select_n | solution.py:49
  63.2 80.8 %all-to-all-done.1 = f32[32,2,64,512]{3,2,1,0:T(8,128)} async-done(((f32[32,2,64,512]{3,2,1,0:T(8,128)}), f32[32,2,64,512]{3,2,1,0:T(8,128)}, u32[]{:S(2)}, u32[]{:S(2)}) %all-to-all-start.1) | async-done | bytes 8388640 | tf_op jit(solution)/shard_map/all_to_all | solution.py:50
  144.0 11.3 %all-to-all-start.2 = ((f32[32,2,512,128]{3,2,1,0:T(8,128)}), f32[32,2,512,128]{3,2,1,0:T(8,128)}, u32[]{:S(2)}, u32[]{:S(2)}) async-start(f32[32,2,512,128]{3,2,1,0:T(8,128)} %broadcast_select_fusion), calls=%async_computation.2 | async-start | bytes 33554432 | tf_op jit(solution)/shard_map/all_to_all | solution.py:51
  171.4 310.4 %all-reduce.3.cloned.1.call-done = (f32[32,64,256]{2,1,0:T(8,128)}, f32[32,256,128]{2,1,0:T(8,128)}) async-done(((f32[32,64,256]{2,1,0:T(8,128)}, f32[32,256,128]{2,1,0:T(8,128)}), (f32[32,64,256]{2,1,0:T(8,128)}, f32[32,256,128]{2,1,0:T(8,128)})) %all-reduce.3.cloned.1.call-update) | async-done | bytes 6291472 | tf_op jit(solution)/shard_map/psum | solution.py:73
  481.8 223.1 %conditional.1 = (f32[12,512,128]{2,1,0:T(8,128)}) conditional(s32[]{:T(128)} %convert_element_type.3, (s32[]{:T(128)}, s32[12,16]{1,0:T(8,128)}, f32[32,2,64,512]{3,2,1,0:T(8,128)}, f32[32,2,512,128]{3,2,1,0:T(8,128)}, f32[64,12,512]{2,1,0:T(8,128)}) %tuple.20, (f32[64,12,512]{2,1,0:T(8,128)}, s32[12,8]{0,1:T(8,128)S(1)}, f32[32,64,256]{2,1,0:T(8,128)}, ...), branch_computations={%region_2.0_spmd, %region_7.13_spmd} | conditional | flops 9687917568 | bytes 60630836 | solution.py:105
  482.5 218.2 %while.19 = (s32[]{:T(128)}, f32[4,512,128]{2,1,0:T(8,128)}, s32[4]{0:T(128)S(1)}, f32[64,12,512]{2,1,0:T(8,128)}, s32[4,16]{1,0:T(4,128)S(1)}, /*index=5*/f32[6...) while((s32[]{:T(128)}, f32[4,512,128]{2,1,0:T(8,128)}, ...), condition=%wide.region_6.7_spmd, body=%wide.region_3.6_spmd.sunk | while | flops 9687917568 | bytes 55387260 | solution.py:88
  490.4 16.2 %fusion.112 = f32[512,16,512]{2,0,1:T(8,128)} fusion(f32[16,64,512]{2,1,0:T(8,128)S(1)} %gather_fusion.3, pred[16]{0:T(512)(128)(4,1)S(1)} %compare_and_fusion.7, f32[64,1,512]{2,1,0:T(1,128)S(1)} %constant_dynamic-slice_fusion.9, pred[]{:T(512)S(6)} %and.57), kind=kOutput, calls=%fused_computation.22.clone.1 | convolution fusion | flops 3221782528 | bytes 19005456 | tf_op jit(solution)/shard_map/cond/branch_0_fun/while/body/eval_jaxpr/dt,jds->tjs/dot_general | solution.py:23
  507.0 8.5 gather_fusion.2
  515.5 21.5 %fusion.114 = f32[4,512,128]{2,1,0:T(8,128)} fusion(f32[4,512,128]{2,1,0:T(8,128)} %get-tuple-element.314, s32[]{:T(128)} %get-tuple-element.313, f32[16,512,128]{2,1,0:T(8,128)} %gather_fusion.2, pred[16]{0:T(512)(128)(4,1)S(1)} %compare_and_fusion.7, f32[512,16,512]{2,0,1:T(8,128)} %fusion.112, f32[16,512]{1,0:T(8,128)S(1)} %multiply_reduce_fusion.5, ...), kind=kOutput, calls=%fused_computation.25.clone.1 | convolution fusion | flops 6464471040 | bytes 21269008 | tf_op jit(solution)/shard_map/cond/branch_0_fun/while/body/eval_jaxpr/tjs,jsw->tw/dot_general | solution.py:28
  545.0 16.2 %fusion.112 = f32[512,16,512]{2,0,1:T(8,128)} fusion(f32[16,64,512]{2,1,0:T(8,128)S(1)} %gather_fusion.3, pred[16]{0:T(512)(128)(4,1)S(1)} %compare_and_fusion.7, f32[64,1,512]{2,1,0:T(1,128)S(1)} %constant_dynamic-slice_fusion.9, pred[]{:T(512)S(6)} %and.57), kind=kOutput, calls=%fused_computation.22.clone.1 | convolution fusion | flops 3221782528 | bytes 19005456 | tf_op jit(solution)/shard_map/cond/branch_0_fun/while/body/eval_jaxpr/dt,jds->tjs/dot_general | solution.py:23
  561.6 8.5 gather_fusion.2
  570.1 21.5 %fusion.114 = f32[4,512,128]{2,1,0:T(8,128)} fusion(f32[4,512,128]{2,1,0:T(8,128)} %get-tuple-element.314, s32[]{:T(128)} %get-tuple-element.313, f32[16,512,128]{2,1,0:T(8,128)} %gather_fusion.2, pred[16]{0:T(512)(128)(4,1)S(1)} %compare_and_fusion.7, f32[512,16,512]{2,0,1:T(8,128)} %fusion.112, f32[16,512]{1,0:T(8,128)S(1)} %multiply_reduce_fusion.5, ...), kind=kOutput, calls=%fused_computation.25.clone.1 | convolution fusion | flops 6464471040 | bytes 21269008 | tf_op jit(solution)/shard_map/cond/branch_0_fun/while/body/eval_jaxpr/tjs,jsw->tw/dot_general | solution.py:28
  599.5 16.2 %fusion.112 = f32[512,16,512]{2,0,1:T(8,128)} fusion(f32[16,64,512]{2,1,0:T(8,128)S(1)} %gather_fusion.3, pred[16]{0:T(512)(128)(4,1)S(1)} %compare_and_fusion.7, f32[64,1,512]{2,1,0:T(1,128)S(1)} %constant_dynamic-slice_fusion.9, pred[]{:T(512)S(6)} %and.57), kind=kOutput, calls=%fused_computation.22.clone.1 | convolution fusion | flops 3221782528 | bytes 19005456 | tf_op jit(solution)/shard_map/cond/branch_0_fun/while/body/eval_jaxpr/dt,jds->tjs/dot_general | solution.py:23
  616.1 8.5 gather_fusion.2
  624.6 21.5 %fusion.114 = f32[4,512,128]{2,1,0:T(8,128)} fusion(f32[4,512,128]{2,1,0:T(8,128)} %get-tuple-element.314, s32[]{:T(128)} %get-tuple-element.313, f32[16,512,128]{2,1,0:T(8,128)} %gather_fusion.2, pred[16]{0:T(512)(128)(4,1)S(1)} %compare_and_fusion.7, f32[512,16,512]{2,0,1:T(8,128)} %fusion.112, f32[16,512]{1,0:T(8,128)S(1)} %multiply_reduce_fusion.5, ...), kind=kOutput, calls=%fused_computation.25.clone.1 | convolution fusion | flops 6464471040 | bytes 21269008 | tf_op jit(solution)/shard_map/cond/branch_0_fun/while/body/eval_jaxpr/tjs,jsw->tw/dot_general | solution.py:28
  654.1 16.2 %fusion.112 = f32[512,16,512]{2,0,1:T(8,128)} fusion(f32[16,64,512]{2,1,0:T(8,128)S(1)} %gather_fusion.3, pred[16]{0:T(512)(128)(4,1)S(1)} %compare_and_fusion.7, f32[64,1,512]{2,1,0:T(1,128)S(1)} %constant_dynamic-slice_fusion.9, pred[]{:T(512)S(6)} %and.57), kind=kOutput, calls=%fused_computation.22.clone.1 | convolution fusion | flops 3221782528 | bytes 19005456 | tf_op jit(solution)/shard_map/cond/branch_0_fun/while/body/eval_jaxpr/dt,jds->tjs/dot_general | solution.py:23
  670.7 8.5 gather_fusion.2
  679.2 21.5 %fusion.114 = f32[4,512,128]{2,1,0:T(8,128)} fusion(f32[4,512,128]{2,1,0:T(8,128)} %get-tuple-element.314, s32[]{:T(128)} %get-tuple-element.313, f32[16,512,128]{2,1,0:T(8,128)} %gather_fusion.2, pred[16]{0:T(512)(128)(4,1)S(1)} %compare_and_fusion.7, f32[512,16,512]{2,0,1:T(8,128)} %fusion.112, f32[16,512]{1,0:T(8,128)S(1)} %multiply_reduce_fusion.5, ...), kind=kOutput, calls=%fused_computation.25.clone.1 | convolution fusion | flops 6464471040 | bytes 21269008 | tf_op jit(solution)/shard_map/cond/branch_0_fun/while/body/eval_jaxpr/tjs,jsw->tw/dot_general | solution.py:28
  705.4 68.3 %collective-permute-done = f32[12,512,128]{2,1,0:T(8,128)S(1)} collective-permute-done((f32[12,512,128]{2,1,0:T(8,128)}, f32[12,512,128]{2,1,0:T(8,128)S(1)}, u32[]{:S(2)}, u32[]{:S(2)}) %collective-permute-start) | collective-permute-done | bytes 3145760 | tf_op jit(solution)/shard_map/ppermute | solution.py:12
  776.0 33.6 %collective-permute-start.1 = (f32[12,512,128]{2,1,0:T(8,128)S(1)}, f32[12,512,128]{2,1,0:T(8,128)S(1)}, u32[]{:S(2)}, u32[]{:S(2)}) collective-permute-start(f32[12,512,128]{2,1,0:T(8,128)S(1)} %add.160), channel_id=1, source_target_pairs={{0,64},{32,96},{64,0},{96,32},{1,65},{33,97},{65,1},{97,33},{2,66}... | collective-permute-start | bytes 9437192 | tf_op jit(solution)/shard_map/ppermute | solution.py:12
  809.6 67.6 %collective-permute-done.1 = f32[12,512,128]{2,1,0:T(8,128)S(1)} collective-permute-done((f32[12,512,128]{2,1,0:T(8,128)S(1)}, f32[12,512,128]{2,1,0:T(8,128)S(1)}, u32[]{:S(2)}, u32[]{:S(2)}) %collective-permute-start.1) | collective-permute-done | bytes 3145760 | tf_op jit(solution)/shard_map/ppermute | solution.py:12
  (77 shorter events, 71.3 us)
Async XLA Ops:
  6.5 37.7 %copy-start = (f32[6144,128]{1,0:T(8,128)S(1)}, f32[6144,128]{1,0:T(8,128)}, u32[]{:S(2)}) copy-start(f32[6144,128]{1,0:T(8,128)} %param.16) | copy-start | bytes 9437188
  8.1 16.4 %all-to-all-start = ((s32[32,1,2]{2,1,0:T(1,128)}), s32[32,1,2]{2,1,0:T(1,128)S(1)}, u32[]{:S(2)}, u32[]{:S(2)}) async-start(s32[32,1,2]{2,1,0:T(1,128)} %copy.36), calls=%async_computation | async-start | bytes 32768 | tf_op jit(solution)/shard_map/all_to_all | solution.py:47
  39.1 105.0 %all-to-all-start.1 = ((f32[32,2,64,512]{3,2,1,0:T(8,128)}), f32[32,2,64,512]{3,2,1,0:T(8,128)}, u32[]{:S(2)}, u32[]{:S(2)}) async-start(f32[32,2,64,512]{3,2,1,0:T(8,128)} %broadcast_select_fusion.1), calls=%async_computation.1 | async-start | bytes 16777216 | tf_op jit(solution)/shard_map/all_to_all | solution.py:50
  144.0 337.8 %all-to-all-start.2 = ((f32[32,2,512,128]{3,2,1,0:T(8,128)}), f32[32,2,512,128]{3,2,1,0:T(8,128)}, u32[]{:S(2)}, u32[]{:S(2)}) async-start(f32[32,2,512,128]{3,2,1,0:T(8,128)} %broadcast_select_fusion), calls=%async_computation.2 | async-start | bytes 33554432 | tf_op jit(solution)/shard_map/all_to_all | solution.py:51
  155.3 3.3 copy-start.4
  155.3 326.5 %all-reduce.3.cloned.1.call-start = ((), (), s32[]{:S(2)}) async-start(), calls=%async_computation.3 | async-start | bytes 12582912 | tf_op jit(solution)/shard_map/psum | solution.py:73
  167.3 2.2 copy-start.2
  169.5 312.3 %copy-start.3 = (s32[12,8]{0,1:T(8,128)S(1)}, s32[12,8]{0,1:T(8,128)}, u32[]{:S(2)}) copy-start(s32[12,8]{0,1:T(8,128)} %param.20) | copy-start | bytes 1156
  705.0 68.7 %collective-permute-start = (f32[12,512,128]{2,1,0:T(8,128)}, f32[12,512,128]{2,1,0:T(8,128)S(1)}, u32[]{:S(2)}, u32[]{:S(2)}) collective-permute-start(f32[12,512,128]{2,1,0:T(8,128)} %get-tuple-element.337), channel_id=1, source_target_pairs={{0,32},{32,0},{64,96},{96,64},{1,33},{33,1},{65,97},{97,65},{2,34}... | collective-permute-start | bytes 9437192 | tf_op jit(solution)/shard_map/ppermute | solution.py:12
  773.7 105.5 %copy-start.1 = (f32[6144,128]{1,0:T(8,128)S(1)}, f32[6144,128]{1,0:T(8,128)}, u32[]{:S(2)}) copy-start(f32[6144,128]{1,0:T(8,128)} %param.16) | copy-start | bytes 9437188
  776.0 101.2 %collective-permute-start.1 = (f32[12,512,128]{2,1,0:T(8,128)S(1)}, f32[12,512,128]{2,1,0:T(8,128)S(1)}, u32[]{:S(2)}, u32[]{:S(2)}) collective-permute-start(f32[12,512,128]{2,1,0:T(8,128)S(1)} %add.160), channel_id=1, source_target_pairs={{0,64},{32,96},{64,0},{96,32},{1,65},{33,97},{65,1},{97,33},{2,66}... | collective-permute-start | bytes 9437192 | tf_op jit(solution)/shard_map/ppermute | solution.py:12
Sparse Core Ops, SparseCore 0:
  169.6 312.1 all-reduce.2
